TPU v7x, 512 devices: a whole 4x4x16 slice. The times are simulated.
512 devices in a mesh: rx: 16 (over z_hi, x, core), ry: 4 (over y), tp: 8 (over z_lo).
Axes of the slice: x: 4, y: 4, z: 16 (z_hi: 2, z_lo: 8; z = z_hi * 8 + z_lo), core: 2. Of those that a mesh axis runs over, the one named last changes fastest.
Arguments:
- weights: bfloat16 [16, 4, 3, 160, 4096], P('rx', 'ry', None, 'tp'), may hold values from -6 to 6
- tracker: bfloat16 [16, 4, 3, 160, 4096], P('rx', 'ry', None, 'tp'), may hold values from -6 to 6
- acts: bfloat16 [16, 4, 1024, 4096], P('rx', 'ry', 'tp'), may hold values from -6 to 6
- cotangent: bfloat16 [16, 4, 1024, 4096], P('rx', 'ry', 'tp'), may hold values from -6 to 6
Outputs:
- new_weights: bfloat16 [16, 4, 3, 160, 4096], P('rx', 'ry', None, 'tp')
- new_tracker: bfloat16 [16, 4, 3, 160, 4096], P('rx', 'ry', None, 'tp')
All inputs are finite; a program needn't handle non-finite values.
Results may differ from a plain program's by a relative error of at most 0.019.
Values may be sent and summed in bfloat16 or wider, within the bound.
A program may use at most 128 MiB of HBM per device.

v0:
```python
import jax
import jax.numpy as jnp
from jax import lax
from jax.sharding import PartitionSpec as P

learning_rate = 0.1


def padded_2(cells, sides, width):
    for axis, dim in sides:
        count = lax.axis_size(axis)
        head = lax.slice_in_dim(cells, 0, width, axis=dim)
        tail = lax.slice_in_dim(cells, cells.shape[dim] - width, cells.shape[dim], axis=dim)
        cells = jnp.concatenate(
            [
                lax.ppermute(tail, axis, [(i, (i + 1) % count) for i in range(count)]),
                cells,
                lax.ppermute(head, axis, [((i + 1) % count, i) for i in range(count)]),
            ],
            axis=dim,
        )
    return cells


def torus_mean(padded):

    def piece(first, second):
        return padded[first, second].astype(jnp.float32)

    total = piece(1, 1) + piece(0, 1) + piece(2, 1) + piece(1, 0) + piece(1, 2)
    return total / 5.0


def forward_backward(token_rows, cotangent_rows, slab_block, input_scale, output_scale):
    both_pre = (
        jnp.einsum("td,khd->kth", token_rows, slab_block[0:2], preferred_element_type=jnp.float32)
        * input_scale
    )
    gate_pre = both_pre[0]
    up_pre = both_pre[1]
    sigmoid_gate = jax.nn.sigmoid(gate_pre)
    gated = gate_pre * sigmoid_gate
    hidden = (gated * up_pre).astype(jnp.bfloat16)
    hidden_grad = (
        jnp.einsum("td,hd->th", cotangent_rows, slab_block[2], preferred_element_type=jnp.float32)
        * output_scale
    )
    up_grad = (hidden_grad * gated).astype(jnp.bfloat16)
    gate_grad = (
        hidden_grad * up_pre * sigmoid_gate * (1.0 + gate_pre * (1.0 - sigmoid_gate))
    ).astype(jnp.bfloat16)
    return (gate_grad, up_grad, hidden)


def on_device(weights, tracker, acts, cotangent):
    own_weights = weights[0, 0]
    own_tracker = tracker[0, 0]
    token_rows = acts[0, 0]
    cotangent_rows = cotangent[0, 0]
    model_width = token_rows.shape[1]
    own_rows = own_weights.shape[1]
    group_count = lax.axis_size("tp")
    input_scale = model_width ** (-0.5)
    output_scale = (own_rows * group_count) ** (-0.5)
    whole_tokens, whole_cotangent = (
        lax.all_gather(token_rows, "tp", axis=0, tiled=True),
        lax.all_gather(cotangent_rows, "tp", axis=0, tiled=True),
    )
    gate_grad, up_grad, hidden = forward_backward(
        whole_tokens, whole_cotangent, own_weights, input_scale, output_scale
    )
    group_rows = token_rows.shape[0]

    def grouped(values):
        return values.reshape(group_count, group_rows, values.shape[1])

    tokens_grouped = grouped(whole_tokens)
    cotangent_grouped = grouped(whole_cotangent)
    paired_grads = jnp.stack([grouped(gate_grad), grouped(up_grad)], axis=0)
    paired_terms = (
        jnp.einsum(
            "kgth,gtd->kghd", paired_grads, tokens_grouped, preferred_element_type=jnp.float32
        )
        * input_scale
    )
    down_term = (
        jnp.einsum(
            "gth,gtd->ghd", grouped(hidden), cotangent_grouped, preferred_element_type=jnp.float32
        )
        * output_scale
    )
    terms = jnp.concatenate([paired_terms, down_term[None]], axis=0).astype(jnp.bfloat16)
    gradient = jnp.sum(terms.astype(jnp.float32), axis=1).astype(jnp.bfloat16)
    gradient_block = gradient[None, None]
    joined = jnp.concatenate([weights, tracker, gradient_block], axis=2)
    padded = padded_2(joined, (("rx", 0), ("ry", 1)), 1)
    all_means = torus_mean(padded)
    weight_mean = all_means[0:3]
    tracker_mean = all_means[3:6]
    gradient_mean = all_means[6:9]
    own_gradient = gradient.astype(jnp.float32)
    tracked = own_tracker.astype(jnp.float32) + own_gradient
    new_weights = (weight_mean - learning_rate * tracked).astype(jnp.bfloat16)
    new_tracker = (tracker_mean + gradient_mean - own_gradient).astype(jnp.bfloat16)
    return (new_weights[None, None], new_tracker[None, None])


def solution(mesh):
    in_specs = (
        P("rx", "ry", None, "tp", None),
        P("rx", "ry", None, "tp", None),
        P("rx", "ry", "tp", None),
        P("rx", "ry", "tp", None),
    )
    out_specs = (P("rx", "ry", None, "tp", None), P("rx", "ry", None, "tp", None))
    return jax.shard_map(
        on_device, mesh=mesh, in_specs=in_specs, out_specs=out_specs, check_vma=False
    )
```

profile of v0, /device:TPU:39, one launch (start us, length us, event | category | flops | bytes accessed | tf_op | source)
XLA Modules:
  0.0 565.1 jit_solution(5520072937437981216)
XLA Ops:
  7.2 0.0 all-gather.7.cloned.1.call-start
  7.2 0.7 all-gather.7.cloned.1.call-update
  7.9 0.0 all-gather.5.cloned.1.call-start
  7.9 0.7 all-gather.5.cloned.1.call-update
  8.6 0.0 copy-start
  8.7 178.9 %all-gather.7.cloned.1.call-done = bf16[1,1,1024,4096]{3,2,1,0:T(8,128)(2,1)} async-done(((bf16[1,1,128,4096]{3,2,1,0:T(8,128)(2,1)}), bf16[1,1,1024,4096]{3,2,1,0:T(8,128)(2,1)}) %all-gather.7.cloned.1.call-update) | async-done | bytes 8388624 | tf_op jit(solution)/shard_map/all_gather | solution.py:66
  187.6 6.2 %fusion.15 = f32[2,1024,20]{1,2,0:T(8,128)S(1)} fusion(bf16[1,1,1024,4096]{3,2,1,0:T(8,128)(2,1)} %all-gather.7.cloned.1.call-done, bf16[1,1,3,20,4096]{4,3,2,1,0:T(8,128)(2,1)} %param.4), kind=kOutput, calls=%fused_computation.23 | convolution fusion | flops 335585280 | bytes 8945664 | tf_op jit(solution)/shard_map/td,khd->kth/dot_general | solution.py:36
  193.8 173.6 %all-gather.5.cloned.1.call-done = bf16[1,1,1024,4096]{3,2,1,0:T(8,128)(2,1)} async-done(((bf16[1,1,128,4096]{3,2,1,0:T(8,128)(2,1)}), bf16[1,1,1024,4096]{3,2,1,0:T(8,128)(2,1)}) %all-gather.5.cloned.1.call-update) | async-done | bytes 8388624 | tf_op jit(solution)/shard_map/all_gather | solution.py:67
  367.4 0.0 copy-done
  367.4 0.0 slice-start
  367.4 5.8 %fusion.35 = (bf16[1024,20]{0,1:T(8,128)(2,1)S(1)}, bf16[1024,20]{0,1:T(8,128)(2,1)S(1)}) fusion(f32[2,1024,20]{1,2,0:T(8,128)S(1)} %fusion.15, bf16[1,1,3,20,4096]{4,3,2,1,0:T(8,128)(2,1)S(1)} %copy-done, bf16[1,1,1024,4096]{3,2,1,0:T(8,128)(2,1)} %all-gather.5.cloned.1.call-done), kind=kOutput, calls=%fused_computation.42 | convolution fusion | flops 168058880 | bytes 8863744 | tf_op jit(solution)/shard_map/td,hd->th/dot_general | solution.py:45
  373.4 0.0 slice-start.1
  373.4 4.7 fusion.6
  378.1 0.0 slice-done
  378.2 0.0 slice-done.1
  378.2 1.2 fusion.4
  379.4 0.0 copy-start.1
  379.4 1.5 maximum_reduce_fusion
  380.9 0.0 copy-done.1
  380.9 0.2 pad_maximum_fusion.1
  381.1 14.0 %collective-permute-start = (bf16[1,1,9,20,4096]{4,3,2,1,0:T(8,128)(2,1)S(1)}, bf16[1,1,9,20,4096]{4,3,2,1,0:T(8,128)(2,1)S(1)}, u32[]{:S(2)}, u32[]{:S(2)}) collective-permute-start(bf16[1,1,9,20,4096]{4,3,2,1,0:T(8,128)(2,1)S(1)} %pad_maximum_fusion.1), channel_id=1, source_target_pairs={{0,32},{32,64},{64,96},{96,128},{128,160},{160,192},{192,224},{224... | collective-permute-start | bytes 4423688 | tf_op jit(solution)/shard_map/ppermute | solution.py:16
  395.1 1.9 collective-permute-start.1
  397.0 74.9 %collective-permute-done = bf16[1,1,9,20,4096]{4,3,2,1,0:T(8,128)(2,1)S(1)} collective-permute-done((bf16[1,1,9,20,4096]{4,3,2,1,0:T(8,128)(2,1)S(1)}, bf16[1,1,9,20,4096]{4,3,2,1,0:T(8,128)(2,1)S(1)}, u32[]{:S(2)}, u32[]{:S(2)}) %collective-permute-start) | collective-permute-done | bytes 1474592 | tf_op jit(solution)/shard_map/ppermute | solution.py:16
  472.0 0.0 collective-permute-done.1
  472.0 1.5 pad_maximum_fusion
  473.5 19.5 %collective-permute-start.3 = (bf16[3,1,9,20,4096]{4,3,2,1,0:T(8,128)(2,1)S(1)}, bf16[3,1,9,20,4096]{4,3,2,1,0:T(8,128)(2,1)S(1)}, u32[]{:S(2)}, u32[]{:S(2)}) collective-permute-start(bf16[3,1,9,20,4096]{4,3,2,1,0:T(8,128)(2,1)S(1)} %pad_maximum_fusion), channel_id=1, source_target_pairs={{8,0},{16,8},{24,16},{0,24},{9,1},{17,9},{25,17},{1,25},{10,2},{18... | collective-permute-start | bytes 13271048 | tf_op jit(solution)/shard_map/ppermute | solution.py:18
  493.0 1.9 collective-permute-start.2
  494.9 55.4 %collective-permute-done.3 = bf16[3,1,9,20,4096]{4,3,2,1,0:T(8,128)(2,1)S(1)} collective-permute-done((bf16[3,1,9,20,4096]{4,3,2,1,0:T(8,128)(2,1)S(1)}, bf16[3,1,9,20,4096]{4,3,2,1,0:T(8,128)(2,1)S(1)}, u32[]{:S(2)}, u32[]{:S(2)}) %collective-permute-start.3) | collective-permute-done | bytes 4423712 | tf_op jit(solution)/shard_map/ppermute | solution.py:18
  550.4 5.0 collective-permute-done.2
  555.4 1.5 add_multiply_fusion
  556.9 1.4 fusion.21
  (11 shorter events, 0.1 us)
Async XLA Ops:
  7.2 180.4 %all-gather.7.cloned.1.call-start = ((), (), s32[]{:S(2)}) async-start(), calls=%async_computation.1 | async-start | bytes 9437184 | tf_op jit(solution)/shard_map/all_gather | solution.py:66
  7.9 359.5 %all-gather.5.cloned.1.call-start = ((), (), s32[]{:S(2)}) async-start(), calls=%async_computation | async-start | bytes 9437184 | tf_op jit(solution)/shard_map/all_gather | solution.py:67
  8.6 358.7 %copy-start = (bf16[1,1,3,20,4096]{4,3,2,1,0:T(8,128)(2,1)S(1)}, bf16[1,1,3,20,4096]{4,3,2,1,0:T(8,128)(2,1)}, u32[]{:S(2)}) copy-start(bf16[1,1,3,20,4096]{4,3,2,1,0:T(8,128)(2,1)} %param.4) | copy-start | bytes 1474564
  367.4 10.8 %slice-start = ((s8[8388608]{0:T(1024)(128)(4,1)}), s8[4194304]{0:T(1024)(128)(4,1)S(1)}, s32[]{:S(2)}) async-start(s8[8388608]{0:T(1024)(128)(4,1)} %bitcast.129), calls=%async_computation.2 | async-start | bytes 8388608
  373.4 4.8 slice-start.1
  379.4 1.5 copy-start.1
  381.1 90.8 %collective-permute-start = (bf16[1,1,9,20,4096]{4,3,2,1,0:T(8,128)(2,1)S(1)}, bf16[1,1,9,20,4096]{4,3,2,1,0:T(8,128)(2,1)S(1)}, u32[]{:S(2)}, u32[]{:S(2)}) collective-permute-start(bf16[1,1,9,20,4096]{4,3,2,1,0:T(8,128)(2,1)S(1)} %pad_maximum_fusion.1), channel_id=1, source_target_pairs={{0,32},{32,64},{64,96},{96,128},{128,160},{160,192},{192,224},{224... | collective-permute-start | bytes 4423688 | tf_op jit(solution)/shard_map/ppermute | solution.py:16
  395.1 76.9 %collective-permute-start.1 = (bf16[1,1,9,20,4096]{4,3,2,1,0:T(8,128)(2,1)S(1)}, bf16[1,1,9,20,4096]{4,3,2,1,0:T(8,128)(2,1)S(1)}, u32[]{:S(2)}, u32[]{:S(2)}) collective-permute-start(bf16[1,1,9,20,4096]{4,3,2,1,0:T(8,128)(2,1)S(1)} %pad_maximum_fusion.1), channel_id=1, source_target_pairs={{32,0},{64,32},{96,64},{128,96},{160,128},{192,160},{224,192},{256... | collective-permute-start | bytes 4423688 | tf_op jit(solution)/shard_map/ppermute | solution.py:18
  473.5 76.8 %collective-permute-start.3 = (bf16[3,1,9,20,4096]{4,3,2,1,0:T(8,128)(2,1)S(1)}, bf16[3,1,9,20,4096]{4,3,2,1,0:T(8,128)(2,1)S(1)}, u32[]{:S(2)}, u32[]{:S(2)}) collective-permute-start(bf16[3,1,9,20,4096]{4,3,2,1,0:T(8,128)(2,1)S(1)} %pad_maximum_fusion), channel_id=1, source_target_pairs={{8,0},{16,8},{24,16},{0,24},{9,1},{17,9},{25,17},{1,25},{10,2},{18... | collective-permute-start | bytes 13271048 | tf_op jit(solution)/shard_map/ppermute | solution.py:18
  493.0 62.4 %collective-permute-start.2 = (bf16[3,1,9,20,4096]{4,3,2,1,0:T(8,128)(2,1)S(1)}, bf16[3,1,9,20,4096]{4,3,2,1,0:T(8,128)(2,1)S(1)}, u32[]{:S(2)}, u32[]{:S(2)}) collective-permute-start(bf16[3,1,9,20,4096]{4,3,2,1,0:T(8,128)(2,1)S(1)} %pad_maximum_fusion), channel_id=1, source_target_pairs={{0,8},{8,16},{16,24},{24,0},{1,9},{9,17},{17,25},{25,1},{2,10},{10... | collective-permute-start | bytes 13271048 | tf_op jit(solution)/shard_map/ppermute | solution.py:16
Sparse Core Ops, SparseCore 0:
  10.1 177.4 all-gather.6
  189.7 177.6 all-gather.4
where the time goes:
time: 565 us
  waiting for transfers between devices  489 us (87%)
  starting transfers between devices  37.3 us (7%)
  matrix products  18 us (3%)
  between operations  14.3 us (3%)
  other arithmetic  6.16 us (1%)
    all_gather x1, waiting for transfers between devices, on_device(): lax.all_gather(token_rows, 'tp', axis=0, tiled=True)  179 us
    all_gather x1, waiting for transfers between devices, on_device(): lax.all_gather(cotangent_rows, 'tp', axis=0, tiled=True)  174 us
    ppermute x2, waiting for transfers between devices, padded_2(): lax.ppermute(tail, axis, [(i, (i + 1) % count) for i in range(count)])  80 us
    ppermute x2, waiting for transfers between devices, padded_2(): lax.ppermute(head, axis, [((i + 1) % count, i) for i in range(count)])  55.4 us
    ppermute x2, starting transfers between devices, padded_2(): lax.ppermute(head, axis, [((i + 1) % count, i) for i in range(count)])  21.4 us
    ppermute x2, starting transfers between devices, padded_2(): lax.ppermute(tail, axis, [(i, (i + 1) % count) for i in range(count)])  15.9 us
  transfers between devices with their start and end apart: 6, of which 5 were waited for; matrix products, arithmetic and copies ran while one was open for 1% of the time, Pallas kernels for 0%

commit v1 on v0

v1 whole, which is shorter than its diff:
```python
import functools

import jax
import jax.numpy as jnp
from jax import lax
from jax.experimental import pallas as pl
from jax.experimental.pallas import tpu as pltpu
from jax.sharding import PartitionSpec as P

MESH = pl.DeviceIdType.MESH

learning_rate = 0.1
chunks = 4
hop_slots = 2
first_slot = 1
far_slot = 2


def kernel(
    sizes,
    scales,
    part_rows,
    acts_hbm,
    cotangent_hbm,
    weights_hbm,
    tracker_hbm,
    new_weights_ref,
    new_tracker_ref,
    tokens,
    blocks,
    partials,
    from_left,
    from_right,
    tracker,
    gradient,
    outgoing,
    near_weights,
    near_tracked,
    load_sem,
    block_recv,
    block_send,
    own_send,
    left_recv,
    left_send,
    right_recv,
    right_send,
    mix_recv,
    mix_send,
    tracked_recv,
    tracked_send,
):
    n_rx, n_ry, n_tp = sizes
    input_scale, output_scale = scales
    rx = lax.axis_index("rx")
    ry = lax.axis_index("ry")
    me = lax.axis_index("tp")
    last = n_tp - 1
    has_left = me > 0
    has_right = me < last
    torus = (
        (lax.rem(rx + 1, n_rx), ry, me),
        (lax.rem(rx + n_rx - 1, n_rx), ry, me),
        (rx, lax.rem(ry + 1, n_ry), me),
        (rx, lax.rem(ry + n_ry - 1, n_ry), me),
    )
    to_left = (rx, ry, me - 1)
    to_right = (rx, ry, me + 1)
    here = (rx, ry, me)

    barrier = pltpu.get_barrier_semaphore()
    for partner in torus:
        pl.semaphore_signal(barrier, inc=1, device_id=partner, device_id_type=MESH)

    @pl.when(has_left)
    def _():
        pl.semaphore_signal(barrier, inc=1, device_id=to_left, device_id_type=MESH)

    @pl.when(has_right)
    def _():
        pl.semaphore_signal(barrier, inc=1, device_id=to_right, device_id_type=MESH)

    token_rows = acts_hbm.shape[0]
    loads = (
        pltpu.make_async_copy(weights_hbm, blocks.at[me], load_sem.at[0]),
        pltpu.make_async_copy(acts_hbm, tokens.at[pl.ds(0, token_rows)], load_sem.at[1]),
        pltpu.make_async_copy(cotangent_hbm, tokens.at[pl.ds(token_rows, token_rows)], load_sem.at[2]),
        pltpu.make_async_copy(tracker_hbm, tracker, load_sem.at[3]),
    )
    for load in loads:
        load.start()

    def send(source, target, send_sem, recv_sem, device):
        return pltpu.make_async_remote_copy(
            src_ref=source,
            dst_ref=target,
            send_sem=send_sem,
            recv_sem=recv_sem,
            device_id=device,
            device_id_type=MESH,
        )

    def block_copy(j, c, device):
        block = blocks.at[j, c]
        return send(block, block, block_send.at[j, c], block_recv.at[j, c], device)

    def own_copy(c):
        block = blocks.at[me, c]
        return send(block, block, own_send.at[c], block_recv.at[me, c], to_left)

    def rightward(j, c, device):
        block = from_left.at[j, c]
        return send(block, block, left_send.at[j, c], left_recv.at[j, c], device)

    def leftward(j, c, device):
        block = from_right.at[j, c]
        return send(block, block, right_send.at[j, c], right_recv.at[j, c], device)

    def mix_copy(k, device):
        return send(blocks.at[me], near_weights.at[k ^ 1], mix_send.at[k], mix_recv.at[k ^ 1], device)

    def tracked_copy(k, c, device):
        return send(
            outgoing.at[c], near_tracked.at[k ^ 1, c], tracked_send.at[k, c], tracked_recv.at[k ^ 1, c], device
        )

    loads[0].wait()
    pl.semaphore_wait(barrier, 4 + has_left.astype(jnp.int32) + has_right.astype(jnp.int32))

    for c in range(chunks):

        @pl.when(has_left)
        def _():
            own_copy(c).start()

        @pl.when(has_right)
        def _():
            block_copy(me, c, to_right).start()

    for k in (2, 3, 0, 1):
        mix_copy(k, torus[k]).start()

    for load in loads[1:]:
        load.wait()

    width = blocks.shape[3]
    rows = blocks.shape[2]
    row = lax.broadcasted_iota(jnp.int32, (rows, token_rows), 0)
    is_gate = row < part_rows
    is_up = (row >= part_rows) & (row < 2 * part_rows)
    is_down = (row >= 2 * part_rows) & (row < 3 * part_rows)
    row_scale = jnp.where(
        lax.broadcasted_iota(jnp.int32, (rows, 1), 0) < 2 * part_rows, input_scale, output_scale
    ).astype(jnp.float32)

    def compute(j):
        pre = jnp.zeros((rows, 2 * token_rows), jnp.float32)
        for c in range(chunks):
            pre += lax.dot_general(
                blocks[j, c],
                tokens[:, c * width : (c + 1) * width],
                (((1,), (1,)), ((), ())),
                preferred_element_type=jnp.float32,
            )
        gate = pre[:, :token_rows] * input_scale
        up = pltpu.roll(pre[:, :token_rows], rows - part_rows, 0) * input_scale
        hidden_grad = pltpu.roll(pre[:, token_rows:], rows - 2 * part_rows, 0) * output_scale
        sigmoid_gate = jax.nn.sigmoid(gate)
        gated = gate * sigmoid_gate
        hidden = gated * up
        up_grad = hidden_grad * gated
        gate_grad = hidden_grad * up * sigmoid_gate * (1.0 + gate * (1.0 - sigmoid_gate))
        with_tokens = jnp.where(is_gate, gate_grad, jnp.where(is_up, pltpu.roll(up_grad, part_rows, 0), 0.0))
        with_cotangent = jnp.where(is_down, pltpu.roll(hidden, 2 * part_rows, 0), 0.0)
        both = jnp.concatenate([with_tokens, with_cotangent], axis=1).astype(jnp.bfloat16)
        for c in range(chunks):
            partials[j, c] = (
                jnp.dot(both, tokens[:, c * width : (c + 1) * width], preferred_element_type=jnp.float32) * row_scale
            )

    start_right = first_slot + (chunks + hop_slots) * me
    start_left = first_slot + (chunks + hop_slots) * (last - me)
    finish = jnp.maximum(start_right, start_left)

    @pl.loop(0, first_slot + (chunks + hop_slots) * last + chunks)
    def _(slot):
        arrived = slot - first_slot + chunks
        distance = lax.div(arrived, chunks)
        c = lax.rem(arrived, chunks)

        @pl.when((distance >= 1) & (me + distance <= last))
        def _():
            j = me + distance
            block_copy(j, c, here).wait_recv()

            @pl.when(has_left)
            def _():
                block_copy(j, c, to_left).start()

        @pl.when((distance >= 1) & (me - distance >= 0))
        def _():
            j = me - distance
            block_copy(j, c, here).wait_recv()

            @pl.when(has_right)
            def _():
                block_copy(j, c, to_right).start()

        @pl.when((c == chunks - 1) & (distance <= last))
        def _():
            @pl.loop(0, 2)
            def _(side):
                j = me + distance * (1 - 2 * side)

                @pl.when((j >= 0) & (j <= last) & (distance + 1 > side))
                def _():
                    compute(j)

        gone = slot - start_right + chunks
        ahead = lax.div(gone, chunks) - 1
        part = lax.rem(gone, chunks)

        @pl.when((gone >= 0) & (ahead >= 1) & (me + ahead <= last))
        def _():
            j = me + ahead

            @pl.when(has_left)
            def _():
                rightward(j, part, here).wait_recv()
                from_left[j, part] = (from_left[j, part].astype(jnp.float32) + partials[j, part]).astype(jnp.bfloat16)

            @pl.when(jnp.logical_not(has_left))
            def _():
                from_left[j, part] = partials[j, part].astype(jnp.bfloat16)

            rightward(j, part, to_right).start()

        gone_left = slot - start_left + chunks
        behind = lax.div(gone_left, chunks) - 1
        piece = lax.rem(gone_left, chunks)

        @pl.when((gone_left >= 0) & (behind >= 1) & (me - behind >= 0))
        def _():
            j = me - behind

            @pl.when(has_right)
            def _():
                leftward(j, piece, here).wait_recv()
                from_right[j, piece] = (from_right[j, piece].astype(jnp.float32) + partials[j, piece]).astype(
                    jnp.bfloat16
                )

            @pl.when(jnp.logical_not(has_right))
            def _():
                from_right[j, piece] = partials[j, piece].astype(jnp.bfloat16)

            leftward(j, piece, to_left).start()

        done = slot - finish

        @pl.when((done >= 0) & (done < chunks))
        def _():
            @pl.when(has_left)
            def _():
                rightward(me, done, here).wait_recv()
                partials[me, done] = partials[me, done] + from_left[me, done].astype(jnp.float32)

            @pl.when(has_right)
            def _():
                leftward(me, done, here).wait_recv()
                partials[me, done] = partials[me, done] + from_right[me, done].astype(jnp.float32)

            rounded = partials[me, done].astype(jnp.bfloat16)
            gradient[done] = rounded
            outgoing[done] = (tracker[done].astype(jnp.float32) + rounded.astype(jnp.float32)).astype(jnp.bfloat16)
            for k in range(4):
                tracked_copy(k, done, torus[k]).start()

    for k in range(4):
        mix_copy(k ^ 1, here).wait_recv()

    @pl.loop(0, chunks)
    def _(c):
        for k in range(4):
            tracked_copy(k ^ 1, c, here).wait_recv()
        own_gradient = gradient[c].astype(jnp.float32)
        tracked = tracker[c].astype(jnp.float32) + own_gradient
        weight_sum = blocks[me, c].astype(jnp.float32)
        tracked_sum = tracked
        for k in range(4):
            weight_sum = weight_sum + near_weights[k, c].astype(jnp.float32)
            tracked_sum = tracked_sum + near_tracked[k, c].astype(jnp.float32)
        new_weights_ref[c] = (weight_sum * 0.2 - learning_rate * tracked).astype(jnp.bfloat16)
        new_tracker_ref[c] = (tracked_sum * 0.2 - own_gradient).astype(jnp.bfloat16)

    for k in range(4):
        mix_copy(k, torus[k]).wait_send()

    @pl.loop(0, chunks)
    def _(c):
        for k in range(4):
            tracked_copy(k, c, torus[k]).wait_send()

        @pl.when(has_left)
        def _():
            own_copy(c).wait_send()

        @pl.when(has_right)
        def _():
            block_copy(me, c, here).wait_send()

        @pl.loop(0, n_tp)
        def _(j):
            @pl.when(((j > me) & has_left) | ((j < me) & has_right))
            def _():
                block_copy(j, c, here).wait_send()

            @pl.when(j > me)
            def _():
                rightward(j, c, here).wait_send()

            @pl.when(j < me)
            def _():
                leftward(j, c, here).wait_send()


def on_device(sizes, weights, tracker, acts, cotangent):
    _, _, matrices, part_rows, model_width = weights.shape
    n_tp = sizes[2]
    used = matrices * part_rows
    rows = -(-used // 16) * 16
    width = model_width // chunks
    token_rows = acts.shape[2]

    def packed(values):
        flat = values.reshape(used, chunks, width)
        flat = jnp.pad(flat, ((0, rows - used), (0, 0), (0, 0)))
        return flat.transpose(1, 0, 2)

    def unpacked(values):
        return values.transpose(1, 0, 2)[:used].reshape(weights.shape)

    scales = (model_width ** (-0.5), (part_rows * n_tp) ** (-0.5))
    shape = (chunks, rows, width)
    half = jnp.bfloat16
    dma = pltpu.SemaphoreType.DMA
    new_weights, new_tracker = pl.pallas_call(
        functools.partial(kernel, sizes, scales, part_rows),
        out_shape=[jax.ShapeDtypeStruct(shape, half)] * 2,
        in_specs=[pl.BlockSpec(memory_space=pl.ANY)] * 4,
        out_specs=[pl.BlockSpec(memory_space=pltpu.VMEM)] * 2,
        scratch_shapes=[
            pltpu.VMEM((2 * token_rows, model_width), half),
            pltpu.VMEM((n_tp, *shape), half),
            pltpu.VMEM((n_tp, *shape), jnp.float32),
            pltpu.VMEM((n_tp, *shape), half),
            pltpu.VMEM((n_tp, *shape), half),
            pltpu.VMEM(shape, half),
            pltpu.VMEM(shape, half),
            pltpu.VMEM(shape, half),
            pltpu.VMEM((4, *shape), half),
            pltpu.VMEM((4, *shape), half),
            dma((4,)),
            dma((n_tp, chunks)),
            dma((n_tp, chunks)),
            dma((chunks,)),
            dma((n_tp, chunks)),
            dma((n_tp, chunks)),
            dma((n_tp, chunks)),
            dma((n_tp, chunks)),
            dma((4,)),
            dma((4,)),
            dma((4, chunks)),
            dma((4, chunks)),
        ],
        compiler_params=pltpu.CompilerParams(
            collective_id=0, has_side_effects=True, vmem_limit_bytes=48 * 1024 * 1024
        ),
        cost_estimate=pl.CostEstimate(flops=2_000_000_000, bytes_accessed=8_000_000, transcendentals=100_000),
    )(acts[0, 0], cotangent[0, 0], packed(weights), packed(tracker))
    return unpacked(new_weights), unpacked(new_tracker)


def solution(mesh):
    sizes = tuple(mesh.shape[axis] for axis in ("rx", "ry", "tp"))
    rows_split = P("rx", "ry", None, "tp", None)
    tokens_split = P("rx", "ry", "tp", None)
    return jax.shard_map(
        functools.partial(on_device, sizes),
        mesh=mesh,
        in_specs=(rows_split, rows_split, tokens_split, tokens_split),
        out_specs=(rows_split, rows_split),
        check_vma=False,
    )
```

time: 565 us -> 208 us (0.37)
  the two profiles are of different devices: /device:TPU:39 before, /device:TPU:31 now
where the time goes in v1:
time: 208 us; the launch traced here: 207 us
  Pallas kernels  199 us (96%)
  local copies, waits for them, and re-layouts  7.47 us (4%)
    pallas_call x1, Pallas kernels, on_device(): pl.pallas_call(functools.partial(kernel, sizes, scales, part_rows), out_s...  199 us

profile of v1, /device:TPU:31, one launch (start us, length us, event | category | flops | bytes accessed | tf_op | source)
XLA Modules:
  0.0 207.4 jit_solution(13407323452082928833)
XLA Ops:
  0.6 1.4 reshape.16
  2.0 0.0 copy-start.2
  2.0 0.2 copy.6
  2.2 0.9 copy-done.2
  3.1 0.3 reshape.17
  3.4 0.2 copy.7
  3.6 0.0 copy-start
  3.6 0.0 copy-start.1
  3.6 0.1 pad_bitcast_fusion
  3.7 1.1 copy-done
  4.8 0.3 copy-done.1
  5.1 199.2 %shard_map.59 = (bf16[4,64,1024]{2,1,0:T(8,128)(2,1)S(1)}, bf16[4,64,1024]{2,1,0:T(8,128)(2,1)S(1)}) custom-call(bf16[128,4096]{1,0:T(8,128)(2,1)S(1)} %bitcast.12, bf16[128,4096]{1,0:T(8,128)(2,1)S(1)} %bitcast.13, bf16[4,64,1024]{2,1,0:T(8,128)(2,1)S(1)} %get-tuple-element.7.weights_hbm, bf16[4,64,1024]{2,1,0:T(8,128)(2,1)S(1)} %get-tuple-element.6.tracker_hbm), custom_call_target="tpu_custom_call" | custom-call | flops 2000000000 | bytes 8000000 | tf_op jit(solution)/shard_map/pallas_call | solution.py:346
  204.4 0.4 copy.8
  204.8 0.4 copy.9
  205.1 1.1 reshape.19
  206.3 1.1 reshape.18
Async XLA Ops:
  2.0 1.1 copy-start.2
  3.6 1.2 copy-start
  3.6 1.5 copy-start.1

commit v2 on v1

--- a/solution.py
+++ b/solution.py
@@ -10,10 +10,9 @@
 MESH = pl.DeviceIdType.MESH
 
 learning_rate = 0.1
-chunks = 4
-hop_slots = 2
+chunks = 8
+hop_slots = 3
 first_slot = 1
-far_slot = 2
 
 
 def kernel(
@@ -31,6 +30,7 @@
     partials,
     from_left,
     from_right,
+    to_far,
     tracker,
     gradient,
     outgoing,
@@ -48,6 +48,9 @@
     mix_send,
     tracked_recv,
     tracked_send,
+    far_weights_recv,
+    far_recv,
+    far_send,
 ):
     n_rx, n_ry, n_tp = sizes
     input_scale, output_scale = scales
@@ -67,9 +70,26 @@
     to_right = (rx, ry, me + 1)
     here = (rx, ry, me)
 
+    place = lax.rem(rx, n_rx // 2)
+    is_first = place == 0
+    is_last = place == n_rx // 2 - 1
+    is_edge = is_first | is_last
+    near = (jnp.logical_not(is_last), jnp.logical_not(is_first), rx >= 0, rx >= 0)
+    far_rx = jnp.where(is_last, torus[0][0], torus[1][0])
+    far_side = jnp.where(is_last, 0, 1)
+    middle = n_tp // 2
+    feeder = (far_rx, ry, jnp.where(me < middle, last, 0))
+
     barrier = pltpu.get_barrier_semaphore()
-    for partner in torus:
-        pl.semaphore_signal(barrier, inc=1, device_id=partner, device_id_type=MESH)
+    for exists, partner in zip(near, torus):
+
+        @pl.when(exists)
+        def _():
+            pl.semaphore_signal(barrier, inc=1, device_id=partner, device_id_type=MESH)
+
+    @pl.when(is_edge)
+    def _():
+        pl.semaphore_signal(barrier, inc=1, device_id=feeder, device_id_type=MESH)
 
     @pl.when(has_left)
     def _():
@@ -123,8 +143,37 @@
             outgoing.at[c], near_tracked.at[k ^ 1, c], tracked_send.at[k, c], tracked_recv.at[k ^ 1, c], device
         )
 
+    def far_weights_copy(j, c):
+        return send(
+            blocks.at[j, c],
+            near_weights.at[1 - far_side, c],
+            block_send.at[j, c],
+            far_weights_recv.at[c],
+            (far_rx, ry, j),
+        )
+
+    def far_copy(j, c, device):
+        block = to_far.at[j, c]
+        return send(block, block, far_send.at[j, c], far_recv.at[j, c], device)
+
+    def last_far_copy(j, c):
+        return send(
+            to_far.at[j, c],
+            near_tracked.at[1 - far_side, c],
+            far_send.at[j, c],
+            tracked_recv.at[1 - far_side, c],
+            (far_rx, ry, j),
+        )
+
     loads[0].wait()
-    pl.semaphore_wait(barrier, 4 + has_left.astype(jnp.int32) + has_right.astype(jnp.int32))
+    expected = (
+        jnp.where(is_edge, 3, 4)
+        + jnp.where(has_left, 1, 0)
+        + jnp.where(has_right, 1, 0)
+        + jnp.where(is_edge & (me == 0), n_tp - middle, 0)
+        + jnp.where(is_edge & (me == last), middle, 0)
+    )
+    pl.semaphore_wait(barrier, expected)
 
     for c in range(chunks):
 
@@ -137,7 +186,10 @@
             block_copy(me, c, to_right).start()
 
     for k in (2, 3, 0, 1):
-        mix_copy(k, torus[k]).start()
+
+        @pl.when(near[k])
+        def _():
+            mix_copy(k, torus[k]).start()
 
     for load in loads[1:]:
         load.wait()
@@ -196,6 +248,10 @@
             def _():
                 block_copy(j, c, to_left).start()
 
+            @pl.when(is_edge & jnp.logical_not(has_left) & (j >= middle))
+            def _():
+                far_weights_copy(j, c).start()
+
         @pl.when((distance >= 1) & (me - distance >= 0))
         def _():
             j = me - distance
@@ -204,6 +260,10 @@
             @pl.when(has_right)
             def _():
                 block_copy(j, c, to_right).start()
+
+            @pl.when(is_edge & jnp.logical_not(has_right) & (j < middle))
+            def _():
+                far_weights_copy(j, c).start()
 
         @pl.when((c == chunks - 1) & (distance <= last))
         def _():
@@ -255,28 +315,71 @@
 
             leftward(j, piece, to_left).start()
 
+        @pl.when(has_left & (gone >= chunks) & (gone < 2 * chunks))
+        def _():
+            rightward(me, part, here).wait_recv()
+            partials[me, part] = partials[me, part] + from_left[me, part].astype(jnp.float32)
+
+        @pl.when(has_right & (gone_left >= chunks) & (gone_left < 2 * chunks))
+        def _():
+            leftward(me, piece, here).wait_recv()
+            partials[me, piece] = partials[me, piece] + from_right[me, piece].astype(jnp.float32)
+
+        @pl.when(is_edge)
+        def _():
+            @pl.loop(0, n_tp)
+            def _(j):
+                goes_right = j < middle
+                hops = jnp.where(goes_right, me - j, j - me)
+                begun = (chunks + hop_slots) * jnp.where(goes_right, j, last - j)
+                at = slot - first_slot - jnp.maximum(begun + hop_slots * hops, chunks * hops)
+
+                @pl.when((hops >= 0) & (at >= 0) & (at < chunks))
+                def _():
+                    @pl.when(hops == 0)
+                    def _():
+                        to_far[j, at] = (tracker[at].astype(jnp.float32) + partials[j, at]).astype(jnp.bfloat16)
+
+                    @pl.when(hops > 0)
+                    def _():
+                        far_copy(j, at, here).wait_recv()
+                        to_far[j, at] = (to_far[j, at].astype(jnp.float32) + partials[j, at]).astype(jnp.bfloat16)
+
+                    ends = jnp.where(goes_right, me == last, me == 0)
+
+                    @pl.when(ends)
+                    def _():
+                        last_far_copy(j, at).start()
+
+                    @pl.when(jnp.logical_not(ends))
+                    def _():
+                        far_copy(j, at, (rx, ry, jnp.where(goes_right, me + 1, me - 1))).start()
+
         done = slot - finish
 
         @pl.when((done >= 0) & (done < chunks))
         def _():
-            @pl.when(has_left)
-            def _():
-                rightward(me, done, here).wait_recv()
-                partials[me, done] = partials[me, done] + from_left[me, done].astype(jnp.float32)
-
-            @pl.when(has_right)
-            def _():
-                leftward(me, done, here).wait_recv()
-                partials[me, done] = partials[me, done] + from_right[me, done].astype(jnp.float32)
-
             rounded = partials[me, done].astype(jnp.bfloat16)
             gradient[done] = rounded
             outgoing[done] = (tracker[done].astype(jnp.float32) + rounded.astype(jnp.float32)).astype(jnp.bfloat16)
-            for k in range(4):
-                tracked_copy(k, done, torus[k]).start()
+            for k in (0, 1, 2, 3):
+
+                @pl.when(near[k])
+                def _():
+                    tracked_copy(k, done, torus[k]).start()
 
     for k in range(4):
-        mix_copy(k ^ 1, here).wait_recv()
+
+        @pl.when(near[k])
+        def _():
+            mix_copy(k ^ 1, here).wait_recv()
+
+    @pl.when(is_edge)
+    def _():
+        @pl.loop(0, chunks)
+        def _(c):
+            landed = near_weights.at[far_side, c]
+            send(landed, landed, far_send.at[0, c], far_weights_recv.at[c], here).wait_recv()
 
     @pl.loop(0, chunks)
     def _(c):
@@ -293,12 +396,18 @@
         new_tracker_ref[c] = (tracked_sum * 0.2 - own_gradient).astype(jnp.bfloat16)
 
     for k in range(4):
-        mix_copy(k, torus[k]).wait_send()
+
+        @pl.when(near[k])
+        def _():
+            mix_copy(k, torus[k]).wait_send()
 
     @pl.loop(0, chunks)
     def _(c):
         for k in range(4):
-            tracked_copy(k, c, torus[k]).wait_send()
+
+            @pl.when(near[k])
+            def _():
+                tracked_copy(k, c, torus[k]).wait_send()
 
         @pl.when(has_left)
         def _():
@@ -310,9 +419,16 @@
 
         @pl.loop(0, n_tp)
         def _(j):
-            @pl.when(((j > me) & has_left) | ((j < me) & has_right))
+            passed = ((j > me) & has_left) | ((j < me) & has_right)
+            farther = ((j >= middle) & (me == 0)) | ((j < middle) & (me == last))
+
+            @pl.when(passed | (is_edge & farther))
             def _():
                 block_copy(j, c, here).wait_send()
+
+            @pl.when(is_edge & (((j < middle) & (j <= me)) | ((j >= middle) & (j >= me))))
+            def _():
+                far_copy(j, c, here).wait_send()
 
             @pl.when(j > me)
             def _():
@@ -354,6 +470,7 @@
             pltpu.VMEM((n_tp, *shape), jnp.float32),
             pltpu.VMEM((n_tp, *shape), half),
             pltpu.VMEM((n_tp, *shape), half),
+            pltpu.VMEM((n_tp, *shape), half),
             pltpu.VMEM(shape, half),
             pltpu.VMEM(shape, half),
             pltpu.VMEM(shape, half),
@@ -371,6 +488,9 @@
             dma((4,)),
             dma((4, chunks)),
             dma((4, chunks)),
+            dma((chunks,)),
+            dma((n_tp, chunks)),
+            dma((n_tp, chunks)),
         ],
         compiler_params=pltpu.CompilerParams(
             collective_id=0, has_side_effects=True, vmem_limit_bytes=48 * 1024 * 1024

time: 208 us -> 185 us (0.89)
  the two profiles are of different devices: /device:TPU:31 before, /device:TPU:8 now
where the time goes in v2:
time: 185 us
  Pallas kernels  177 us (96%)
  local copies, waits for them, and re-layouts  7.17 us (4%)
    pallas_call x1, Pallas kernels, on_device(): pl.pallas_call(functools.partial(kernel, sizes, scales, part_rows), out_s...  177 us

profile of v2, /device:TPU:8, one launch (start us, length us, event | category | flops | bytes accessed | tf_op | source)
XLA Modules:
  0.0 185.2 jit_solution(3302157226529959671)
XLA Ops:
  0.6 1.4 reshape.16
  2.0 0.0 copy-start.2
  2.0 0.1 copy.6
  2.2 0.9 copy-done.2
  3.1 0.3 reshape.17
  3.4 0.1 copy.7
  3.5 0.0 copy-start
  3.5 0.0 copy-start.1
  3.6 0.1 pad_bitcast_fusion
  3.7 1.1 copy-done
  4.8 0.3 copy-done.1
  5.1 177.3 %shard_map.59 = (bf16[8,64,512]{2,1,0:T(8,128)(2,1)S(1)}, bf16[8,64,512]{2,1,0:T(8,128)(2,1)S(1)}) custom-call(bf16[128,4096]{1,0:T(8,128)(2,1)S(1)} %bitcast.12, bf16[128,4096]{1,0:T(8,128)(2,1)S(1)} %bitcast.13, bf16[8,64,512]{2,1,0:T(8,128)(2,1)S(1)} %get-tuple-element.7.weights_hbm, bf16[8,64,512]{2,1,0:T(8,128)(2,1)S(1)} %get-tuple-element.6.tracker_hbm), custom_call_target="tpu_custom_call" | custom-call | flops 2000000000 | bytes 8000000 | tf_op jit(solution)/shard_map/pallas_call | solution.py:462
  182.4 0.3 copy.8
  182.7 0.3 copy.9
  183.0 1.1 reshape.19
  184.1 1.1 reshape.18
Async XLA Ops:
  2.0 1.1 copy-start.2
  3.5 1.2 copy-start
  3.5 1.5 copy-start.1

commit v3 on v2

--- a/solution.py
+++ b/solution.py
@@ -11,8 +11,41 @@
 
 learning_rate = 0.1
 chunks = 8
-hop_slots = 3
-first_slot = 1
+hop_slots = 4
+compute_slots = 2
+arrival_order = (1, 2, 3, 7, 6, 5, 4)
+
+
+def timetable(n_tp):
+    last = n_tp - 1
+    sent, arrived, summed, far = {}, {}, {}, {}
+    for p in range(last, -1, -1):
+        free = 0
+        for j in arrival_order + (0,):
+            if j < p:
+                continue
+            slot = max(free, 0 if j == p else sent[p + 1, j] + hop_slots)
+            if p == 0 and j > 0:
+                slot = sent[1, j] + hop_slots
+            sent[p, j] = slot
+            free = slot + chunks
+    for p in range(n_tp):
+        free = 0
+        for j in arrival_order:
+            if j <= p:
+                continue
+            slot = max(free, sent[p, j] + chunks - 1 + compute_slots)
+            if p > 0:
+                slot = max(slot, summed[p - 1, j] + hop_slots)
+            summed[p, j] = slot
+            free = slot + chunks
+    for j in range(n_tp):
+        summed[j, j] = summed[j - 1, j] + hop_slots if j else 0
+    for j in range(n_tp // 2):
+        far[j, j] = summed[j, j]
+        for p in range(j + 1, n_tp):
+            far[p, j] = max(far[p - 1, j] + hop_slots, sent[last - p, last - j] + chunks - 1 + compute_slots)
+    return sent, summed, far
 
 
 def kernel(
@@ -175,16 +208,6 @@
     )
     pl.semaphore_wait(barrier, expected)
 
-    for c in range(chunks):
-
-        @pl.when(has_left)
-        def _():
-            own_copy(c).start()
-
-        @pl.when(has_right)
-        def _():
-            block_copy(me, c, to_right).start()
-
     for k in (2, 3, 0, 1):
 
         @pl.when(near[k])
@@ -229,136 +252,176 @@
                 jnp.dot(both, tokens[:, c * width : (c + 1) * width], preferred_element_type=jnp.float32) * row_scale
             )
 
-    start_right = first_slot + (chunks + hop_slots) * me
-    start_left = first_slot + (chunks + hop_slots) * (last - me)
-    finish = jnp.maximum(start_right, start_left)
-
-    @pl.loop(0, first_slot + (chunks + hop_slots) * last + chunks)
+    sent, summed, far = timetable(n_tp)
+
+    def at_me(values):
+        chosen = jnp.int32(values[0])
+        for p in range(1, n_tp):
+            chosen = jnp.where(me == p, values[p], chosen)
+        return chosen
+
+    devices = range(n_tp)
+    own_left = at_me([sent[p, p] for p in devices])
+    own_right = at_me([sent[last - p, last - p] for p in devices])
+    arrives = [at_me([sent[p, j] if j > p else sent[last - p, last - j] for p in devices]) for j in devices]
+    leaves = [at_me([summed[p, j] if j > p else summed[last - p, last - j] for p in devices]) for j in devices]
+    far_leaves = [
+        at_me([far.get((p, j) if j < middle else (last - p, last - j), -chunks) for p in devices]) for j in devices
+    ]
+    right_ends = at_me([summed[p, p] for p in devices])
+    left_ends = at_me([summed[last - p, last - p] for p in devices])
+    finish = jnp.maximum(right_ends, left_ends)
+    slots = max(max(table.values()) for table in (sent, summed, far)) + chunks
+
+    @pl.loop(0, slots)
     def _(slot):
-        arrived = slot - first_slot + chunks
-        distance = lax.div(arrived, chunks)
-        c = lax.rem(arrived, chunks)
-
-        @pl.when((distance >= 1) & (me + distance <= last))
-        def _():
-            j = me + distance
-            block_copy(j, c, here).wait_recv()
-
-            @pl.when(has_left)
-            def _():
-                block_copy(j, c, to_left).start()
-
-            @pl.when(is_edge & jnp.logical_not(has_left) & (j >= middle))
-            def _():
-                far_weights_copy(j, c).start()
-
-        @pl.when((distance >= 1) & (me - distance >= 0))
-        def _():
-            j = me - distance
-            block_copy(j, c, here).wait_recv()
-
-            @pl.when(has_right)
-            def _():
-                block_copy(j, c, to_right).start()
-
-            @pl.when(is_edge & jnp.logical_not(has_right) & (j < middle))
-            def _():
-                far_weights_copy(j, c).start()
-
-        @pl.when((c == chunks - 1) & (distance <= last))
+        c_left = slot - own_left
+        c_right = slot - own_right
+
+        @pl.when(has_left & (c_left >= 0) & (c_left < chunks))
+        def _():
+            own_copy(c_left).start()
+
+        @pl.when(has_right & (c_right >= 0) & (c_right < chunks))
+        def _():
+            block_copy(me, c_right, to_right).start()
+
+        full_right = jnp.where(slot == 0, me, -1)
+        full_left = jnp.int32(-1)
+        for j in range(n_tp):
+            c = slot - arrives[j]
+            full = c == chunks - 1
+            if j > 0:
+                full_right = jnp.where(full & (j > me), j, full_right)
+
+                @pl.when((j > me) & (c >= 0) & (c < chunks))
+                def _():
+                    block_copy(j, c, here).wait_recv()
+
+                    @pl.when(has_left)
+                    def _():
+                        block_copy(j, c, to_left).start()
+
+                    if j >= middle:
+
+                        @pl.when(is_edge & jnp.logical_not(has_left))
+                        def _():
+                            far_weights_copy(j, c).start()
+
+            if j < last:
+                full_left = jnp.where(full & (j < me), j, full_left)
+
+                @pl.when((j < me) & (c >= 0) & (c < chunks))
+                def _():
+                    block_copy(j, c, here).wait_recv()
+
+                    @pl.when(has_right)
+                    def _():
+                        block_copy(j, c, to_right).start()
+
+                    if j < middle:
+
+                        @pl.when(is_edge & jnp.logical_not(has_right))
+                        def _():
+                            far_weights_copy(j, c).start()
+
+        @pl.when((full_right >= 0) | (full_left >= 0))
         def _():
             @pl.loop(0, 2)
             def _(side):
-                j = me + distance * (1 - 2 * side)
-
-                @pl.when((j >= 0) & (j <= last) & (distance + 1 > side))
+                j = jnp.where(side == 0, full_right, full_left)
+
+                @pl.when(j >= 0)
                 def _():
                     compute(j)
 
-        gone = slot - start_right + chunks
-        ahead = lax.div(gone, chunks) - 1
-        part = lax.rem(gone, chunks)
-
-        @pl.when((gone >= 0) & (ahead >= 1) & (me + ahead <= last))
-        def _():
-            j = me + ahead
-
-            @pl.when(has_left)
-            def _():
-                rightward(j, part, here).wait_recv()
-                from_left[j, part] = (from_left[j, part].astype(jnp.float32) + partials[j, part]).astype(jnp.bfloat16)
-
-            @pl.when(jnp.logical_not(has_left))
-            def _():
-                from_left[j, part] = partials[j, part].astype(jnp.bfloat16)
-
-            rightward(j, part, to_right).start()
-
-        gone_left = slot - start_left + chunks
-        behind = lax.div(gone_left, chunks) - 1
-        piece = lax.rem(gone_left, chunks)
-
-        @pl.when((gone_left >= 0) & (behind >= 1) & (me - behind >= 0))
-        def _():
-            j = me - behind
-
-            @pl.when(has_right)
-            def _():
-                leftward(j, piece, here).wait_recv()
-                from_right[j, piece] = (from_right[j, piece].astype(jnp.float32) + partials[j, piece]).astype(
-                    jnp.bfloat16
-                )
-
-            @pl.when(jnp.logical_not(has_right))
-            def _():
-                from_right[j, piece] = partials[j, piece].astype(jnp.bfloat16)
-
-            leftward(j, piece, to_left).start()
-
-        @pl.when(has_left & (gone >= chunks) & (gone < 2 * chunks))
+        for j in range(n_tp):
+            c = slot - leaves[j]
+            if j > 0:
+
+                @pl.when((j > me) & (c >= 0) & (c < chunks))
+                def _():
+                    @pl.when(has_left)
+                    def _():
+                        rightward(j, c, here).wait_recv()
+                        from_left[j, c] = (from_left[j, c].astype(jnp.float32) + partials[j, c]).astype(jnp.bfloat16)
+
+                    @pl.when(jnp.logical_not(has_left))
+                    def _():
+                        from_left[j, c] = partials[j, c].astype(jnp.bfloat16)
+
+                    rightward(j, c, to_right).start()
+
+            if j < last:
+
+                @pl.when((j < me) & (c >= 0) & (c < chunks))
+                def _():
+                    @pl.when(has_right)
+                    def _():
+                        leftward(j, c, here).wait_recv()
+                        from_right[j, c] = (from_right[j, c].astype(jnp.float32) + partials[j, c]).astype(
+                            jnp.bfloat16
+                        )
+
+                    @pl.when(jnp.logical_not(has_right))
+                    def _():
+                        from_right[j, c] = partials[j, c].astype(jnp.bfloat16)
+
+                    leftward(j, c, to_left).start()
+
+        part = slot - right_ends
+        piece = slot - left_ends
+
+        @pl.when(has_left & (part >= 0) & (part < chunks))
         def _():
             rightward(me, part, here).wait_recv()
-            partials[me, part] = partials[me, part] + from_left[me, part].astype(jnp.float32)
-
-        @pl.when(has_right & (gone_left >= chunks) & (gone_left < 2 * chunks))
+
+        @pl.when(has_right & (piece >= 0) & (piece < chunks))
         def _():
             leftward(me, piece, here).wait_recv()
-            partials[me, piece] = partials[me, piece] + from_right[me, piece].astype(jnp.float32)
 
         @pl.when(is_edge)
         def _():
-            @pl.loop(0, n_tp)
-            def _(j):
+            for j in range(n_tp):
+                at = slot - far_leaves[j]
                 goes_right = j < middle
-                hops = jnp.where(goes_right, me - j, j - me)
-                begun = (chunks + hop_slots) * jnp.where(goes_right, j, last - j)
-                at = slot - first_slot - jnp.maximum(begun + hop_slots * hops, chunks * hops)
-
-                @pl.when((hops >= 0) & (at >= 0) & (at < chunks))
-                def _():
-                    @pl.when(hops == 0)
-                    def _():
-                        to_far[j, at] = (tracker[at].astype(jnp.float32) + partials[j, at]).astype(jnp.bfloat16)
-
-                    @pl.when(hops > 0)
+                below = j <= me if goes_right else j >= me
+                end = last if goes_right else 0
+
+                @pl.when(below & (at >= 0) & (at < chunks))
+                def _():
+                    @pl.when(me == j)
+                    def _():
+                        begun = tracker[at].astype(jnp.float32) + partials[j, at]
+                        if 0 < j < last:
+                            begun = begun + (from_left if goes_right else from_right)[j, at].astype(jnp.float32)
+                        to_far[j, at] = begun.astype(jnp.bfloat16)
+
+                    @pl.when(me != j)
                     def _():
                         far_copy(j, at, here).wait_recv()
                         to_far[j, at] = (to_far[j, at].astype(jnp.float32) + partials[j, at]).astype(jnp.bfloat16)
 
-                    ends = jnp.where(goes_right, me == last, me == 0)
-
-                    @pl.when(ends)
+                    @pl.when(me == end)
                     def _():
                         last_far_copy(j, at).start()
 
-                    @pl.when(jnp.logical_not(ends))
-                    def _():
-                        far_copy(j, at, (rx, ry, jnp.where(goes_right, me + 1, me - 1))).start()
+                    @pl.when(me != end)
+                    def _():
+                        far_copy(j, at, to_right if goes_right else to_left).start()
 
         done = slot - finish
 
         @pl.when((done >= 0) & (done < chunks))
         def _():
+            @pl.when(has_left)
+            def _():
+                partials[me, done] = partials[me, done] + from_left[me, done].astype(jnp.float32)
+
+            @pl.when(has_right)
+            def _():
+                partials[me, done] = partials[me, done] + from_right[me, done].astype(jnp.float32)
+
             rounded = partials[me, done].astype(jnp.bfloat16)
             gradient[done] = rounded
             outgoing[done] = (tracker[done].astype(jnp.float32) + rounded.astype(jnp.float32)).astype(jnp.bfloat16)

time: 185 us -> 175 us (0.946)
  the two profiles are of different devices: /device:TPU:8 before, /device:TPU:96 now
where the time goes in v3:
time: 175 us; the launch traced here: 174 us
  Pallas kernels  166 us (95%)
  local copies, waits for them, and re-layouts  7.17 us (4%)
    pallas_call x1, Pallas kernels, on_device(): pl.pallas_call(functools.partial(kernel, sizes, scales, part_rows), out_s...  166 us

profile of v3, /device:TPU:96, one launch (start us, length us, event | category | flops | bytes accessed | tf_op | source)
XLA Modules:
  0.0 174.3 jit_solution(16308280655611510478)
XLA Ops:
  0.6 1.4 reshape.16
  2.0 0.0 copy-start.2
  2.0 0.1 copy.6
  2.2 0.9 copy-done.2
  3.1 0.3 reshape.17
  3.4 0.1 copy.7
  3.5 0.0 copy-start
  3.5 0.0 copy-start.1
  3.6 0.1 pad_bitcast_fusion
  3.7 1.1 copy-done
  4.8 0.3 copy-done.1
  5.1 166.4 %shard_map.59 = (bf16[8,64,512]{2,1,0:T(8,128)(2,1)S(1)}, bf16[8,64,512]{2,1,0:T(8,128)(2,1)S(1)}) custom-call(bf16[128,4096]{1,0:T(8,128)(2,1)S(1)} %bitcast.12, bf16[128,4096]{1,0:T(8,128)(2,1)S(1)} %bitcast.13, bf16[8,64,512]{2,1,0:T(8,128)(2,1)S(1)} %get-tuple-element.7.weights_hbm, bf16[8,64,512]{2,1,0:T(8,128)(2,1)S(1)} %get-tuple-element.6.tracker_hbm), custom_call_target="tpu_custom_call" | custom-call | flops 2000000000 | bytes 8000000 | tf_op jit(solution)/shard_map/pallas_call | solution.py:525
  171.5 0.3 copy.8
  171.8 0.3 copy.9
  172.0 1.1 reshape.19
  173.2 1.1 reshape.18
Async XLA Ops:
  2.0 1.1 copy-start.2
  3.5 1.2 copy-start
  3.5 1.5 copy-start.1

commit v4 on v3

--- a/solution.py
+++ b/solution.py
@@ -11,7 +11,7 @@
 
 learning_rate = 0.1
 chunks = 8
-hop_slots = 4
+hop_slots = 5
 compute_slots = 2
 arrival_order = (1, 2, 3, 7, 6, 5, 4)
 

time: 175 us -> 174 us (level)
  no operation moved by 1% of the time
where the time goes in v4:
time: 174 us
  Pallas kernels  166 us (95%)
  local copies, waits for them, and re-layouts  7.17 us (4%)
    pallas_call x1, Pallas kernels, on_device(): pl.pallas_call(functools.partial(kernel, sizes, scales, part_rows), out_s...  166 us

profile of v4, /device:TPU:96, one launch (start us, length us, event | category | flops | bytes accessed | tf_op | source)
XLA Modules:
  0.0 173.8 jit_solution(6512265287260469693)
XLA Ops:
  0.6 1.4 reshape.16
  2.0 0.0 copy-start.2
  2.0 0.1 copy.6
  2.2 0.9 copy-done.2
  3.1 0.3 reshape.17
  3.4 0.1 copy.7
  3.5 0.0 copy-start
  3.5 0.0 copy-start.1
  3.6 0.1 pad_bitcast_fusion
  3.7 1.1 copy-done
  4.8 0.3 copy-done.1
  5.1 165.9 %shard_map.59 = (bf16[8,64,512]{2,1,0:T(8,128)(2,1)S(1)}, bf16[8,64,512]{2,1,0:T(8,128)(2,1)S(1)}) custom-call(bf16[128,4096]{1,0:T(8,128)(2,1)S(1)} %bitcast.12, bf16[128,4096]{1,0:T(8,128)(2,1)S(1)} %bitcast.13, bf16[8,64,512]{2,1,0:T(8,128)(2,1)S(1)} %get-tuple-element.7.weights_hbm, bf16[8,64,512]{2,1,0:T(8,128)(2,1)S(1)} %get-tuple-element.6.tracker_hbm), custom_call_target="tpu_custom_call" | custom-call | flops 2000000000 | bytes 8000000 | tf_op jit(solution)/shard_map/pallas_call | solution.py:525
  171.0 0.3 copy.8
  171.3 0.3 copy.9
  171.6 1.1 reshape.19
  172.7 1.1 reshape.18
Async XLA Ops:
  2.0 1.1 copy-start.2
  3.5 1.2 copy-start
  3.5 1.5 copy-start.1
